TPU v7x, 768 devices: a whole 4x8x12 slice. The times are simulated.
768 devices in a mesh: dp: 192 (over y, z, core), mp: 4 (over x).
Axes of the slice: x: 4, y: 8, z: 12, core: 2. Of those that a mesh axis runs over, the one named last changes fastest.
Arguments:
- activations: bfloat16 [192, 256, 2048], P('dp'), may hold values from -6 to 6
- output_grads: bfloat16 [192, 256, 2048], P('dp', None, 'mp'), may hold values from -8 to 8, as said below
- error_in: bfloat16 [192, 2048, 2048], P('dp', None, 'mp'), may hold values from -3 to 3
- start_basis: float32 [32, 2048], P(None, 'mp'), may hold values from -6 to 6
Outputs:
- new_error: bfloat16 [192, 2048, 2048], P('dp', None, 'mp')
- update: bfloat16 [2048, 2048], P(None, 'mp')
Inputs may be any that keep to these rules, and one draw needn't show every extreme that they name: `output_grads`: real values.
All inputs are finite; a program needn't handle non-finite values.
Results may differ from a plain program's by a relative error of at most 0.002.
Values sent between devices are 32-bit elements; how exact they have to be, the bound alone decides.
A program may use at most 32 MiB of HBM per device.

v0:
```python
import math

import jax
import jax.numpy as jnp
from jax import lax
from jax.sharding import PartitionSpec as P

clip_scale = 1.5


def cholesky_solve_rows(gram_matrix, left_factor):
    lower_factor = jnp.linalg.cholesky(gram_matrix)
    return lax.linalg.triangular_solve(lower_factor, left_factor, left_side=True, lower=True)


def per_device(activations, output_grads, error_in, start_basis):
    highest = lax.Precision.HIGHEST
    out_width = output_grads.shape[2]
    ranks = start_basis.shape[0]
    replicas = lax.axis_size("dp")
    full_out = out_width * lax.axis_size("mp")
    gradient = lax.dot_general(
        activations[0],
        output_grads[0],
        (((0,), (0,)), ((), ())),
        preferred_element_type=jnp.float32,
    )
    accumulated = gradient + error_in[0].astype(jnp.float32)
    left_term = lax.dot_general(
        start_basis,
        accumulated,
        (((1,), (1,)), ((), ())),
        precision=highest,
        preferred_element_type=jnp.float32,
    )
    left_factor = lax.psum(left_term, ("dp", "mp"))
    gram_matrix = jnp.dot(
        left_factor, left_factor.T, precision=highest, preferred_element_type=jnp.float32
    )
    ortho_basis = cholesky_solve_rows(gram_matrix, left_factor)
    right_term = jnp.dot(
        ortho_basis, accumulated, precision=highest, preferred_element_type=jnp.float32
    )
    right_factor = lax.psum(right_term, "dp")
    squares = lax.psum(jnp.sum(right_factor * right_factor), "mp")
    total_norm = jnp.sqrt(squares)
    limit = clip_scale * math.sqrt(replicas * ranks * full_out)
    ratio = total_norm / limit
    clip_factor = 1.0 / jnp.sqrt(1.0 + ratio * ratio)
    decompressed = lax.dot_general(
        ortho_basis,
        right_factor,
        (((0,), (0,)), ((), ())),
        precision=highest,
        preferred_element_type=jnp.float32,
    )
    new_error = (accumulated - decompressed / replicas).astype(jnp.bfloat16)[None]
    update = (clip_factor * decompressed).astype(jnp.bfloat16)
    return (new_error, update)


def solution(mesh):
    in_specs = (P("dp", None, None), P("dp", None, "mp"), P("dp", None, "mp"), P(None, "mp"))
    out_specs = (P("dp", None, "mp"), P(None, "mp"))
    return jax.shard_map(
        per_device, mesh=mesh, in_specs=in_specs, out_specs=out_specs, check_vma=False
    )
```

profile of v0, /device:TPU:1, one launch (start us, length us, event | category | flops | bytes accessed | tf_op | source)
XLA Modules:
  0.0 798.9 jit_solution(11379910248717862710)
XLA Ops:
  7.2 0.0 copy-start
  7.2 0.0 copy-start.2
  7.2 0.0 all-reduce.3.cloned.1.call-start
  7.2 1.2 copy-done
  8.4 2.4 convert_add_fusion
  10.8 0.0 copy-start.1
  10.8 1.9 copy-done.1
  12.8 0.0 copy-done.2
  12.8 4.6 convolution_bitcast_fusion
  17.4 0.0 all-reduce.3.cloned.1.call-update
  17.4 0.0 all-reduce.5.cloned.1.call-start
  17.5 470.6 %all-reduce.3.cloned.1.call-done = f32[32,2048]{1,0:T(8,128)} async-done(((f32[32,2048]{1,0:T(8,128)}), f32[32,2048]{1,0:T(8,128)}) %all-reduce.3.cloned.1.call-update) | async-done | bytes 262160 | tf_op jit(solution)/shard_map/psum | solution.py:36
  488.1 1.4 fusion.7
  489.5 0.1 copy.6
  489.6 2.9 cholesky.16
  492.5 0.6 compare_reduce_fusion
  493.2 0.7 fusion.3
  493.8 2.4 custom-call.6
  496.3 1.4 fusion.4
  497.7 5.3 fusion.8
  503.0 0.0 all-reduce.5.cloned.1.call-update
  503.0 271.0 %all-reduce.5.cloned.1.call-done = f32[32,512]{1,0:T(8,128)} async-done(((f32[32,512]{1,0:T(8,128)}), f32[32,512]{1,0:T(8,128)}) %all-reduce.5.cloned.1.call-update) | async-done | bytes 65552 | tf_op jit(solution)/shard_map/psum | solution.py:44
  774.0 1.5 multiply_reduce_fusion
  775.4 9.0 %psum.23 = f32[]{:T(128)} all-reduce(f32[]{:T(128)} %multiply_reduce_fusion), channel_id=1, replica_groups=mesh['dp'=192,'mp'=4] {'mp'}, use_global_device_ids=true, to_apply=%region_5.6 | all-reduce | flops 1 | bytes 8 | tf_op jit(solution)/shard_map/psum | solution.py:45
  785.2 6.9 multiply_convert_fusion
  (2 shorter events, 0.0 us)
Async XLA Ops:
  7.2 1.2 copy-start
  7.2 5.6 copy-start.2
  7.2 480.9 %all-reduce.3.cloned.1.call-start = ((), (), s32[]{:S(2)}) async-start(), calls=%async_computation | async-start | bytes 524288 | tf_op jit(solution)/shard_map/psum | solution.py:36
  10.8 1.9 copy-start.1
  17.4 756.5 %all-reduce.5.cloned.1.call-start = ((), (), s32[]{:S(2)}) async-start(), calls=%async_computation.1 | async-start | bytes 131072 | tf_op jit(solution)/shard_map/psum | solution.py:44
Sparse Core Ops, SparseCore 0:
  17.5 470.5 all-reduce.2
  503.1 270.8 all-reduce.4
where the time goes:
time: 800 us; the launch traced here: 799 us
  waiting for transfers between devices  742 us (93%)
  matrix products  22 us (3%)
  between operations  14.8 us (2%)
  blocking collectives  9.01 us (1%)
  other arithmetic  8.15 us (1%)
    psum x1, waiting for transfers between devices, per_device(): left_factor = lax.psum(left_term, ('dp', 'mp'))  471 us
    psum x1, waiting for transfers between devices, per_device(): right_factor = lax.psum(right_term, 'dp')  271 us
  transfers between devices with their start and end apart: 2, of which 2 were waited for; matrix products, arithmetic and copies ran while one was open for 0% of the time, Pallas kernels for 0%

commit v1 on v0

v1 whole, which is shorter than its diff:
```python
import functools
import math

import jax
import jax.numpy as jnp
from jax import lax
from jax.experimental import pallas as pl
from jax.experimental.pallas import tpu as pltpu
from jax.sharding import PartitionSpec as P

clip_scale = 1.5

GRID = (8, 12, 2)

MESH = pl.DeviceIdType.MESH
F32 = jnp.float32
BF16 = jnp.bfloat16
LANES = 128
NT = (((1,), (1,)), ((), ()))
NN = (((1,), (0,)), ((), ()))
TN = (((0,), (0,)), ((), ()))
PHASES = 11
A_CORE, A_SPLIT, A_LINE, A_JOIN, A_CORE2, B_CORE, B_SPLIT, B_LINE, B_JOIN, B_CORE2, NORM = range(PHASES)


def dot(a, b, dims):
    return lax.dot_general(a, b, dims, preferred_element_type=F32)


def exact_dot(a, b, dims):
    return lax.dot_general(a, b, dims, precision=lax.Precision.HIGHEST, preferred_element_type=F32)


def pieces(value):
    first = value.astype(BF16)
    rest = value - first.astype(F32)
    second = rest.astype(BF16)
    third = (rest - second.astype(F32)).astype(BF16)
    return first, second, third


def stack(value):
    return jnp.concatenate(pieces(value), axis=0)


def unstack(value):
    rows = value.shape[0] // 3
    return (value[2 * rows :] + value[rows : 2 * rows]) + value[:rows]


def ring_offsets(sizes):
    offsets = [()]
    for size in sizes:
        offsets = [o + (k,) for o in offsets for k in range(size)]
    far = lambda o: sum(min(k, s - k) for k, s in zip(o, sizes))
    return sorted([o for o in offsets if any(o)], key=lambda o: -far(o))


def kernel(
    xs, ys, zs, cs, limit,
    act_hbm, grad_hbm, err_hbm, basis_hbm,
    err_out, upd_out,
    act, grad, err, basis, acc,
    a_term, a_core, a_sum, a_split, a_line, left, left_t,
    b_term, b_core, b_split, b_line, right, norm,
    in_sem, send_sem, recv_sem,
):
    replica, x = lax.axis_index("dp"), lax.axis_index("mp")
    y, z, c = replica // (zs * cs), (replica // cs) % zs, replica % cs
    other = 1 - c
    half_in = act.shape[2]
    half_out = grad.shape[2]
    ranks = basis.shape[0]

    def at(px, py, pz, pc):
        return ((py * zs + pz) * cs + pc, px)

    def load(source, target, k):
        copy = pltpu.make_async_copy(source, target, in_sem.at[k])
        copy.start()
        return copy

    copies = {"basis": load(basis_hbm, basis, 0)}
    for q in range(cs):
        copies["grad", q] = load(grad_hbm.at[0, :, pl.ds(q * half_out, half_out)], grad.at[q], 1 + q)
    k = 1 + cs
    for place, h in enumerate((other, c)):
        cols = pl.ds(pl.multiple_of(h * half_in, LANES), half_in)
        copies["act", place] = load(act_hbm.at[0, :, cols], act.at[h], k)
        rows = pl.ds(pl.multiple_of(h * half_in, LANES), half_in)
        for q in range(cs):
            copies["err", place, q] = load(
                err_hbm.at[0, rows, pl.ds(q * half_out, half_out)], err.at[h, q], k + 1 + q
            )
        k += 1 + cs

    plane = [((x + ox) % xs, (y + oy) % ys) for ox, oy in ring_offsets((xs, ys))]
    column = [(y + oy) % ys for (oy,) in ring_offsets((ys,))]
    line = [(z + oz) % zs for (oz,) in ring_offsets((zs,))]
    row = [(x + ox) % xs for (ox,) in ring_offsets((xs,))]
    partners = [at(px, py, z, c) for px, py in plane] + [at(x, y, pz, c) for pz in line]
    partners += [at(x, y, z, other)]
    barrier = pltpu.get_barrier_semaphore()
    for partner in partners:
        pl.semaphore_signal(barrier, inc=1, device_id=partner, device_id_type=MESH)

    def send(source, target, phase, device):
        pltpu.make_async_remote_copy(
            src_ref=source,
            dst_ref=target,
            send_sem=send_sem.at[phase],
            recv_sem=recv_sem.at[phase],
            device_id=device,
            device_id_type=MESH,
        ).start()

    def arrived(phase, like):
        pltpu.make_async_copy(like, like, recv_sem.at[phase]).wait()

    def sent(phase, like):
        pltpu.make_async_copy(like, like, send_sem.at[phase]).wait()

    copies["basis"].wait()
    basis_parts = [stack(basis[:, q * half_out : (q + 1) * half_out]) for q in range(cs)]
    through = jnp.zeros((3 * ranks, grad.shape[1]), F32)
    for q in range(cs):
        copies["grad", q].wait()
        through += dot(basis_parts[q], grad[q], NT)
    through = stack(unstack(through))

    def left_term(place, h):
        copies["act", place].wait()
        term = dot(through, act[h], NN)
        for q in range(cs):
            copies["err", place, q].wait()
            term += dot(basis_parts[q], err[h, q], NT)
        term = unstack(term)
        width = a_term.shape[4]
        for py in range(ys):
            a_term[h, py] = term[:, py * width : (py + 1) * width].reshape(a_term.shape[2:])

    left_term(0, other)
    pl.semaphore_wait(barrier, len(partners))
    send(a_term.at[other], a_core, A_CORE, at(x, y, z, other))
    left_term(1, c)
    arrived(A_CORE, a_core)
    a_sum[...] = a_term[c] + a_core[...]

    me = y * xs + x
    for px, py in plane:
        send(a_sum.at[py, px], a_split.at[me], A_SPLIT, at(px, py, z, c))
    a_split[me] = a_sum[y, x]

    for h in range(cs):
        for q in range(cs):
            acc[h, q] = dot(act[h], grad[q], TN) + err[h, q].astype(F32)

    arrived(A_SPLIT, a_split.at[pl.ds(0, xs * ys - 1)])
    a_line[z] = jnp.sum(a_split[...], axis=0)
    for pz in line:
        send(a_line.at[z], a_line.at[z], A_LINE, at(x, y, pz, c))
    arrived(A_LINE, a_line.at[pl.ds(0, zs - 1)])
    left[c, y, x] = jnp.sum(a_line[...], axis=0)
    for px, py in plane:
        send(left.at[c, y, x], left.at[c, y, x], A_JOIN, at(px, py, z, c))
    arrived(A_JOIN, a_split.at[pl.ds(0, xs * ys - 1)])
    send(left.at[c], left.at[c], A_CORE2, at(x, y, z, other))
    arrived(A_CORE2, left.at[0])

    left_parts = []
    for h in range(cs):
        blocks = [left[h, py].reshape(ranks, left.shape[4]) for py in range(ys)]
        left_parts.append(pieces(jnp.concatenate(blocks, axis=1)))
    left_stacks = [jnp.concatenate(p, axis=0) for p in left_parts]
    through = jnp.zeros((3 * ranks, grad.shape[1]), F32)
    for h in range(cs):
        through += dot(left_stacks[h], act[h], NT)
    through = stack(unstack(through))

    b_rows = b_term.shape[2]
    b_wide = half_out // LANES

    def right_term(q):
        term = dot(through, grad[q], NN)
        for h in range(cs):
            term += dot(left_stacks[h], err[h, q], NN)
        term = unstack(term)
        for p in range(ys):
            i, j = p // b_wide, p % b_wide
            b_term[q, p] = term[i * b_rows : (i + 1) * b_rows, j * LANES : (j + 1) * LANES]

    right_term(other)
    send(b_term.at[other], b_core, B_CORE, at(x, y, z, other))
    right_term(c)
    arrived(B_CORE, b_core)
    b_core[...] = b_term[c] + b_core[...]
    for py in column:
        send(b_core.at[py], b_split.at[y], B_SPLIT, at(x, py, z, c))
    b_split[y] = b_core[y]

    gram = jnp.zeros((ranks, ranks), F32)
    for first, second, third in left_parts:
        low = dot(jnp.concatenate([first, second], axis=0), second, NT)
        gram += dot(first, third, NT) + dot(third, first, NT)
        gram += low[:ranks] + low[ranks:]
        gram += dot(second, first, NT)
    for first, second, third in left_parts:
        gram += dot(first, first, NT)
    at_row = lax.broadcasted_iota(jnp.int32, (ranks, ranks), 0)
    at_col = lax.broadcasted_iota(jnp.int32, (ranks, ranks), 1)
    inverse = (at_row == at_col).astype(F32)
    for j in range(ranks - 1):
        factor = gram[:, j : j + 1] / gram[j : j + 1, j : j + 1]
        factor = jnp.where(at_row > j, factor, 0.0)
        gram = gram - factor * gram[j : j + 1, :]
        inverse = inverse - factor * inverse[j : j + 1, :]
    pivots = jnp.sum(jnp.where(at_row == at_col, gram, 0.0), axis=1, keepdims=True)
    inverse = inverse / jnp.sqrt(pivots)

    arrived(B_SPLIT, b_split.at[pl.ds(0, ys - 1)])
    b_line[z] = jnp.sum(b_split[...], axis=0)
    for pz in line:
        send(b_line.at[z], b_line.at[z], B_LINE, at(x, y, pz, c))

    for h in range(cs):
        one, two, three = left_parts[h]
        blank = jnp.zeros((2 * ranks, half_in), BF16)
        rows6 = jnp.concatenate([one, one, one, two, two, three, blank], axis=0)
        left_t[h] = rows6.T

    arrived(B_LINE, b_line.at[pl.ds(0, zs - 1)])
    right[c, y] = jnp.sum(b_line[...], axis=0)
    for py in column:
        send(right.at[c, y], right.at[c, y], B_JOIN, at(x, py, z, c))
    arrived(B_JOIN, right.at[0, pl.ds(0, ys - 1)])
    send(right.at[c], right.at[c], B_CORE2, at(x, y, z, other))
    arrived(B_CORE2, right.at[0])

    halves = []
    for q in range(cs):
        lines = [
            jnp.concatenate([right[q, i * b_wide + j] for j in range(b_wide)], axis=1)
            for i in range(ys // b_wide)
        ]
        halves.append(jnp.concatenate(lines, axis=0))
    raw = jnp.concatenate(halves, axis=1)
    factor = exact_dot(inverse, raw, NN)
    squares = jnp.sum((factor * factor).reshape(ranks // 8, 8, cs * half_out), axis=0)
    squares = sum(squares[:, j * LANES : (j + 1) * LANES] for j in range(cs * b_wide))
    norm[x] = squares
    for px in row:
        send(norm.at[x], norm.at[x], NORM, at(px, y, z, c))

    weights = exact_dot(inverse, factor, TN)
    one, two, three = pieces(weights)
    blank = jnp.zeros((2 * ranks, cs * half_out), BF16)
    weights = jnp.concatenate([one, two, three, one, two, one, blank], axis=0)
    replicas = ys * zs * cs
    for h in range(cs):
        for q in range(cs):
            cols = slice(q * half_out, (q + 1) * half_out)
            whole = dot(left_t[h], weights[:, cols], NN)
            err_out[h * half_in : (h + 1) * half_in, cols] = (acc[h, q] - whole / replicas).astype(BF16)
            acc[h, q] = whole

    arrived(NORM, norm.at[pl.ds(0, xs - 1)])
    total = jnp.sum(norm[...], axis=0)
    total = jnp.sum(jnp.sum(total, axis=0, keepdims=True), axis=1, keepdims=True)
    ratio = jnp.sqrt(total) / limit
    clip = 1.0 / jnp.sqrt(1.0 + ratio * ratio)
    for h in range(cs):
        for q in range(cs):
            cols = slice(q * half_out, (q + 1) * half_out)
            upd_out[h * half_in : (h + 1) * half_in, cols] = (clip * acc[h, q]).astype(BF16)

    sent(A_CORE, a_core)
    sent(A_SPLIT, a_split.at[pl.ds(0, xs * ys - 1)])
    sent(A_LINE, a_line.at[pl.ds(0, zs - 1)])
    sent(A_JOIN, a_split.at[pl.ds(0, xs * ys - 1)])
    sent(A_CORE2, left.at[0])
    sent(B_CORE, b_core)
    sent(B_SPLIT, b_split.at[pl.ds(0, ys - 1)])
    sent(B_LINE, b_line.at[pl.ds(0, zs - 1)])
    sent(B_JOIN, right.at[0, pl.ds(0, ys - 1)])
    sent(B_CORE2, right.at[0])
    sent(NORM, norm.at[pl.ds(0, xs - 1)])


def per_device(activations, output_grads, error_in, start_basis):
    ys, zs, cs = GRID
    xs = lax.axis_size("mp")
    tokens, features = activations.shape[1:]
    width = output_grads.shape[2]
    ranks = start_basis.shape[0]
    half_in, half_out = features // cs, width // cs
    limit = clip_scale * math.sqrt(ys * zs * cs * ranks * width * xs)
    a_piece = (ranks // xs, half_in // ys)
    b_piece = (ranks * half_out // ys // LANES, LANES)
    outs = pl.pallas_call(
        functools.partial(kernel, xs, ys, zs, cs, limit),
        out_shape=[pltpu.VMEM((features, width), BF16)] * 2,
        in_specs=[pl.BlockSpec(memory_space=pl.ANY)] * 4,
        out_specs=[pl.BlockSpec(memory_space=pltpu.VMEM)] * 2,
        scratch_shapes=[
            pltpu.VMEM((cs, tokens, half_in), BF16),
            pltpu.VMEM((cs, tokens, half_out), BF16),
            pltpu.VMEM((cs, cs, half_in, half_out), BF16),
            pltpu.VMEM((ranks, width), F32),
            pltpu.VMEM((cs, cs, half_in, half_out), F32),
            pltpu.VMEM((cs, ys, xs) + a_piece, F32),
            pltpu.VMEM((ys, xs) + a_piece, F32),
            pltpu.VMEM((ys, xs) + a_piece, F32),
            pltpu.VMEM((ys * xs,) + a_piece, F32),
            pltpu.VMEM((zs,) + a_piece, F32),
            pltpu.VMEM((cs, ys, xs) + a_piece, F32),
            pltpu.VMEM((cs, half_in, 8 * ranks), BF16),
            pltpu.VMEM((cs, ys) + b_piece, F32),
            pltpu.VMEM((ys,) + b_piece, F32),
            pltpu.VMEM((ys,) + b_piece, F32),
            pltpu.VMEM((zs,) + b_piece, F32),
            pltpu.VMEM((cs, ys) + b_piece, F32),
            pltpu.VMEM((xs, 8, LANES), F32),
            pltpu.SemaphoreType.DMA((1 + cs + cs * (1 + cs),)),
            pltpu.SemaphoreType.DMA((PHASES,)),
            pltpu.SemaphoreType.DMA((PHASES,)),
        ],
        compiler_params=pltpu.CompilerParams(
            collective_id=0, has_side_effects=True, vmem_limit_bytes=58 * 2**20
        ),
        name="compress",
    )(activations, output_grads, error_in, start_basis)
    return outs[0][None], outs[1]


def solution(mesh):
    in_specs = (P("dp", None, None), P("dp", None, "mp"), P("dp", None, "mp"), P(None, "mp"))
    out_specs = (P("dp", None, "mp"), P(None, "mp"))
    return jax.shard_map(
        per_device, mesh=mesh, in_specs=in_specs, out_specs=out_specs, check_vma=False
    )
```

time: 800 us -> 69.6 us (0.09)
  waiting for transfers between devices: 742 us -> 0 us
  Pallas kernels: 0 us -> 66.2 us
  matrix products: 22 us -> 0 us
  between operations: 14.8 us -> 0.64 us
  blocking collectives: 9.01 us -> 0 us
  other arithmetic: 8.15 us -> 0 us
    psum x2 -> x0, waiting for transfers between devices: 742 us -> none  [the longest x1 471 us: per_device(): left_factor = lax.psum(left_term, ('dp', 'mp'))]
    pallas_call x0 -> x1, Pallas kernels: none -> 66.2 us  [per_device(): pl.pallas_call(functools.partial(kernel, xs, ys, zs, cs, limit), out_shap...]
    dot_general x5 -> x0, matrix products: 20.6 us -> none  [the longest x1 6.91 us: per_device(): lax.dot_general(ortho_basis, right_factor, (((0,), (0,)), ((), ())), prec...]
    psum x1 -> x0, blocking collectives: 9.01 us -> none  [per_device(): squares = lax.psum(jnp.sum(right_factor * right_factor), 'mp')]
  transfers between devices with their start and end apart: 2 -> 0, of which waited for: 2 -> 0; matrix products, arithmetic and copies ran while one was open for 0% -> 0% of each run, Pallas kernels for 0% -> 0%
where the time goes in v1:
time: 69.6 us; the launch traced here: 69.5 us
  Pallas kernels  66.2 us (95%)
  local copies, waits for them, and re-layouts  2.64 us (4%)
    pallas_call x1, Pallas kernels, per_device(): pl.pallas_call(functools.partial(kernel, xs, ys, zs, cs, limit), out_shap...  66.2 us
    unnamed x2, local copies, waits for them, and re-layouts  2.64 us

profile of v1, /device:TPU:1, one launch (start us, length us, event | category | flops | bytes accessed | tf_op | source)
XLA Modules:
  0.0 69.5 jit_solution(5383744392543377443)
XLA Ops:
  0.6 66.2 %compress.1 = (bf16[2048,512]{1,0:T(8,128)(2,1)S(1)}, bf16[2048,512]{1,0:T(8,128)(2,1)S(1)}) custom-call(bf16[1,256,2048]{2,1,0:T(8,128)(2,1)} %act_hbm.1, bf16[1,256,512]{2,1,0:T(8,128)(2,1)} %grad_hbm.1, bf16[1,2048,512]{2,1,0:T(8,128)(2,1)} %err_hbm.1, f32[32,512]{1,0:T(8,128)} %basis_hbm.1), custom_call_target="tpu_custom_call" | custom-call | tf_op jit(solution)/shard_map/compress/pallas_call | solution.py:299
  66.9 1.3 %copy.8 = bf16[1,2048,512]{2,1,0:T(8,128)(2,1)} copy(bf16[1,2048,512]{2,1,0:T(8,128)(2,1)S(1)} %bitcast.1) | data formatting | bytes 4194304
  68.2 1.3 %copy.9 = bf16[2048,512]{1,0:T(8,128)(2,1)} copy(bf16[2048,512]{1,0:T(8,128)(2,1)S(1)} %get-tuple-element.7) | data formatting | bytes 4194304

commit v2 on v0

v2 whole, which is shorter than its diff:
```python
import functools
import math

import jax
import jax.numpy as jnp
from jax import lax
from jax.experimental import pallas as pl
from jax.experimental.pallas import tpu as pltpu
from jax.sharding import PartitionSpec as P

clip_scale = 1.5

GRID = (8, 12, 2)

MESH = pl.DeviceIdType.MESH
F32 = jnp.float32
BF16 = jnp.bfloat16
LANES = 128
ROWS = 8
NT = (((1,), (1,)), ((), ()))
NN = (((1,), (0,)), ((), ()))
TN = (((0,), (0,)), ((), ()))
PHASES = 10
A_CORE, A_SPLIT, A_LINE, A_JOIN, A_TWIN, B_SPLIT, B_LINE, B_CORE, B_JOIN, NORM = range(PHASES)


def dot(a, b, dims):
    return lax.dot_general(a, b, dims, preferred_element_type=F32)


def exact_dot(a, b, dims):
    return lax.dot_general(a, b, dims, precision=lax.Precision.HIGHEST, preferred_element_type=F32)


def pieces(value):
    first = value.astype(BF16)
    rest = value - first.astype(F32)
    second = rest.astype(BF16)
    third = (rest - second.astype(F32)).astype(BF16)
    return first, second, third


def stack(value):
    return jnp.concatenate(pieces(value), axis=0)


def unstack(value):
    rows = value.shape[0] // 3
    return (value[2 * rows :] + value[rows : 2 * rows]) + value[:rows]


def pack(value):
    return jnp.concatenate([value[r : r + ROWS] for r in range(0, value.shape[0], ROWS)], axis=1)


def unpack(value, columns):
    return jnp.concatenate([value[:, j : j + columns] for j in range(0, value.shape[1], columns)], axis=0)


def ring(offset, size):
    return min(offset, size - offset)


def ring_offsets(sizes):
    offsets = [()]
    for size in sizes:
        offsets = [o + (k,) for o in offsets for k in range(size)]
    far = lambda o: sum(ring(k, s) for k, s in zip(o, sizes))
    return sorted([o for o in offsets if any(o)], key=lambda o: -far(o))


def reduce_kernel(
    xs, ys, zs, cs, limit,
    act_hbm, grad_hbm, err_hbm, basis_hbm,
    err_out, whole_out, clip_out,
    act, grad, err, basis, acc,
    a_term, a_core, a_split, a_line, left, left_t,
    b_term, b_split, b_line, b_mine, b_core, right, norm,
    in_sem, send_sem, recv_sem,
):
    replica, x = lax.axis_index("dp"), lax.axis_index("mp")
    y, z, c = replica // (zs * cs), (replica // cs) % zs, replica % cs
    ranks, width = basis.shape
    depth = act.shape[2]
    half = depth // cs
    far = ys // 2

    def at(px, py, pz, pc):
        return ((py * zs + pz) * cs + pc, px)

    plane = [((x + ox) % xs, (y + oy) % ys, ring(oy, ys)) for ox, oy in ring_offsets((xs, ys))]
    column = [(y + oy) % ys for (oy,) in ring_offsets((ys,))]
    line = [(z + oz) % zs for (oz,) in ring_offsets((zs,))]
    twin = at(x, y, z, 1 - c)
    partners = [at(x, y, pz, c) for pz in line[:3]] + [at(px, py, z, c) for px, py, _ in plane]
    partners += [at(x, y, pz, c) for pz in line[3:]] + [twin]
    barrier = pltpu.get_barrier_semaphore()
    for partner in partners:
        pl.semaphore_signal(barrier, inc=1, device_id=partner, device_id_type=MESH)

    loads = []

    def load(source, target):
        copy = pltpu.make_async_copy(source, target, in_sem.at[len(loads)])
        copy.start()
        loads.append(copy)

    load(basis_hbm, basis)
    load(grad_hbm.at[0], grad)
    for py in range(ys):
        load(act_hbm.at[0, :, pl.ds(py * depth, depth)], act.at[py])
    for py in range(ys):
        load(err_hbm.at[py], err.at[py])

    def send(source, target, phase, device, arrival=None):
        pltpu.make_async_remote_copy(
            src_ref=source,
            dst_ref=target,
            send_sem=send_sem.at[phase],
            recv_sem=recv_sem.at[phase if arrival is None else arrival],
            device_id=device,
            device_id_type=MESH,
        ).start()

    def arrived(phase, like):
        pltpu.make_async_copy(like, like, recv_sem.at[phase]).wait()

    def sent(phase, like):
        pltpu.make_async_copy(like, like, send_sem.at[phase]).wait()

    loads[0].wait()
    loads[1].wait()
    basis_parts = stack(basis[...])
    through = stack(unstack(dot(basis_parts, grad[...], NT)))
    for py in range(ys):
        loads[2 + py].wait()
        loads[2 + ys + py].wait()
        term = unstack(dot(through, act[py], NN) + dot(basis_parts, err[py], NT))
        for h in range(cs):
            a_term[h, py] = term[:, h * half : (h + 1) * half].reshape(a_term.shape[2:])

    pl.semaphore_wait(barrier, len(partners))
    me = y * xs + x
    send(a_term.at[1 - c], a_core, A_CORE, twin)
    arrived(A_CORE, a_core)
    a_core[...] = a_term[c] + a_core[...]
    for px, py, _ in plane:
        send(a_core.at[py, px], a_split.at[me], A_SPLIT, at(px, py, z, c))
    a_split[me] = a_core[y, x]

    for py in range(ys):
        acc[py] = dot(act[py], grad[...], TN) + err[py].astype(F32)

    others = xs * ys - 1
    arrived(A_SPLIT, a_split.at[pl.ds(0, others)])
    a_line[z] = jnp.sum(a_split[...], axis=0)
    for pz in line:
        send(a_line.at[z], a_line.at[z], A_LINE, at(x, y, pz, c))
    arrived(A_LINE, a_line.at[pl.ds(0, zs - 1)])
    left[c, y, x] = jnp.sum(a_line[...], axis=0)
    for px, py, distance in plane:
        send(left.at[c, y, x], left.at[c, y, x], A_JOIN, at(px, py, z, c), PHASES + distance)

    def left_block(py):
        return jnp.concatenate([left[h, py].reshape(ranks, half) for h in range(cs)], axis=1)

    through = jnp.zeros((3 * ranks, grad.shape[0]), F32)
    term = jnp.zeros((3 * ranks, width), F32)
    for distance in range(far + 2):
        if distance <= far:
            rows = [oy for oy in range(ys) if ring(oy, ys) == distance]
            count = len(rows) * xs - (distance == 0)
            arrived(PHASES + distance, a_split.at[pl.ds(0, count)])
            for oy in rows:
                mine = left.at[c, (y + oy) % ys]
                send(mine, mine, A_TWIN, twin, PHASES + far + 1 + distance)
        if distance > 0:
            rows = [oy for oy in range(ys) if ring(oy, ys) == distance - 1]
            arrived(PHASES + far + distance, a_split.at[pl.ds(0, len(rows) * xs)])
            for oy in rows:
                py = (y + oy) % ys
                block = stack(left_block(py))
                through += dot(block, act[py], NT)
                term += dot(block, err[py], NN)
    term = unstack(term + dot(stack(unstack(through)), grad[...], NN))
    columns = width // ys
    for py in range(ys):
        b_term[py] = pack(term[:, py * columns : (py + 1) * columns])

    for py in column:
        send(b_term.at[py], b_split.at[y], B_SPLIT, at(x, py, z, c))
    b_split[y] = b_term[y]

    gram = jnp.zeros((ranks, ranks), F32)
    for py in range(ys):
        first, second, third = pieces(left_block(py))
        low = dot(jnp.concatenate([first, second], axis=0), second, NT)
        gram += (dot(first, third, NT) + dot(third, first, NT)) + (low[ranks:] + low[:ranks])
        gram += dot(second, first, NT)
        gram += dot(first, first, NT)
    at_row = lax.broadcasted_iota(jnp.int32, (ranks, ranks), 0)
    at_col = lax.broadcasted_iota(jnp.int32, (ranks, ranks), 1)
    inverse = (at_row == at_col).astype(F32)
    for j in range(ranks - 1):
        factor = gram[:, j : j + 1] / gram[j : j + 1, j : j + 1]
        factor = jnp.where(at_row > j, factor, 0.0)
        gram = gram - factor * gram[j : j + 1, :]
        inverse = inverse - factor * inverse[j : j + 1, :]
    pivots = jnp.sum(jnp.where(at_row == at_col, gram, 0.0), axis=1, keepdims=True)
    inverse = inverse / jnp.sqrt(pivots)

    arrived(B_SPLIT, b_split.at[pl.ds(0, ys - 1)])
    b_line[z] = jnp.sum(b_split[...], axis=0)
    for pz in line:
        send(b_line.at[z], b_line.at[z], B_LINE, at(x, y, pz, c))

    for py in range(ys):
        one, two, three = pieces(left_block(py))
        blank = jnp.zeros((2 * ranks, depth), BF16)
        left_t[py] = jnp.concatenate([one, one, one, two, two, three, blank], axis=0).T

    arrived(B_LINE, b_line.at[pl.ds(0, zs - 1)])
    b_mine[...] = jnp.sum(b_line[...], axis=0)
    send(b_mine, b_core, B_CORE, twin)
    arrived(B_CORE, b_core)
    right[y] = b_mine[...] + b_core[...]
    for py in column:
        send(right.at[y], right.at[y], B_JOIN, at(x, py, z, c))

    factor = exact_dot(inverse, unpack(right[y], columns), NN)
    squares = jnp.sum((factor * factor).reshape(ranks // ROWS, ROWS, columns), axis=0)
    if columns < LANES:
        squares = jnp.concatenate([squares, jnp.zeros((ROWS, LANES - columns), F32)], axis=1)
    else:
        squares = sum(squares[:, j : j + LANES] for j in range(0, columns, LANES))
    norm[me] = squares
    for px, py, _ in plane:
        send(norm.at[me], norm.at[me], NORM, at(px, py, z, c))

    arrived(B_JOIN, right.at[pl.ds(0, ys - 1)])
    raw = jnp.concatenate([unpack(right[py], columns) for py in range(ys)], axis=1)
    weights = exact_dot(inverse, exact_dot(inverse, raw, NN), TN)
    one, two, three = pieces(weights)
    blank = jnp.zeros((2 * ranks, width), BF16)
    weights = jnp.concatenate([one, two, three, one, two, one, blank], axis=0)
    replicas = ys * zs * cs
    for py in range(ys):
        whole = dot(left_t[py], weights, NN)
        err_out[py] = (acc[py] - whole / replicas).astype(BF16)
        whole_out[py] = whole

    arrived(NORM, norm.at[pl.ds(0, others)])
    total = jnp.sum(norm[...], axis=0)
    total = jnp.sum(jnp.sum(total, axis=0, keepdims=True), axis=1, keepdims=True)
    ratio = jnp.sqrt(total) / limit
    clip_out[...] = jnp.broadcast_to(1.0 / jnp.sqrt(1.0 + ratio * ratio), clip_out.shape)

    sent(A_CORE, a_core)
    sent(A_SPLIT, a_split.at[pl.ds(0, others)])
    sent(A_LINE, a_line.at[pl.ds(0, zs - 1)])
    sent(A_JOIN, a_split.at[pl.ds(0, others)])
    sent(A_TWIN, left.at[0])
    sent(B_SPLIT, b_split.at[pl.ds(0, ys - 1)])
    sent(B_LINE, b_line.at[pl.ds(0, zs - 1)])
    sent(B_CORE, b_core)
    sent(B_JOIN, right.at[pl.ds(0, ys - 1)])
    sent(NORM, norm.at[pl.ds(0, others)])


def write_kernel(err_in, whole, clip, err_hbm, upd_hbm, upd, sem):
    blocks, depth, width = whole.shape
    copies = []

    def store(source, target):
        copies.append(pltpu.make_async_copy(source, target, sem.at[len(copies)]))
        copies[-1].start()

    for k in range(blocks):
        store(err_in.at[k], err_hbm.at[0, pl.ds(k * depth, depth)])
    scale = clip[:1, :1]
    for k in range(blocks):
        upd[k] = (scale * whole[k]).astype(BF16)
        store(upd.at[k], upd_hbm.at[pl.ds(k * depth, depth)])
    for copy in copies:
        copy.wait()


def per_device(activations, output_grads, error_in, start_basis):
    ys, zs, cs = GRID
    xs = lax.axis_size("mp")
    tokens, features = activations.shape[1:]
    width = output_grads.shape[2]
    ranks = start_basis.shape[0]
    depth = features // ys
    limit = clip_scale * math.sqrt(ys * zs * cs * ranks * width * xs)
    a_piece = (ranks // xs, depth // cs)
    b_piece = (ROWS, ranks // ROWS * (width // ys))
    in_vmem = pl.BlockSpec(memory_space=pltpu.VMEM)
    in_hbm = pl.BlockSpec(memory_space=pl.ANY)
    new_error, whole, clip = pl.pallas_call(
        functools.partial(reduce_kernel, xs, ys, zs, cs, limit),
        out_shape=[
            pltpu.VMEM((ys, depth, width), BF16),
            pltpu.VMEM((ys, depth, width), F32),
            pltpu.VMEM((ROWS, LANES), F32),
        ],
        in_specs=[in_hbm] * 4,
        out_specs=[in_vmem] * 3,
        scratch_shapes=[
            pltpu.VMEM((ys, tokens, depth), BF16),
            pltpu.VMEM((tokens, width), BF16),
            pltpu.VMEM((ys, depth, width), BF16),
            pltpu.VMEM((ranks, width), F32),
            pltpu.VMEM((ys, depth, width), F32),
            pltpu.VMEM((cs, ys, xs) + a_piece, F32),
            pltpu.VMEM((ys, xs) + a_piece, F32),
            pltpu.VMEM((ys * xs,) + a_piece, F32),
            pltpu.VMEM((zs,) + a_piece, F32),
            pltpu.VMEM((cs, ys, xs) + a_piece, F32),
            pltpu.VMEM((ys, depth, 8 * ranks), BF16),
            pltpu.VMEM((ys,) + b_piece, F32),
            pltpu.VMEM((ys,) + b_piece, F32),
            pltpu.VMEM((zs,) + b_piece, F32),
            pltpu.VMEM(b_piece, F32),
            pltpu.VMEM(b_piece, F32),
            pltpu.VMEM((ys,) + b_piece, F32),
            pltpu.VMEM((ys * xs, ROWS, LANES), F32),
            pltpu.SemaphoreType.DMA((2 + 2 * ys,)),
            pltpu.SemaphoreType.DMA((PHASES,)),
            pltpu.SemaphoreType.DMA((PHASES + 2 * (ys // 2 + 1),)),
        ],
        compiler_params=pltpu.CompilerParams(
            collective_id=0, has_side_effects=True, vmem_limit_bytes=56 * 2**20
        ),
        name="reduce",
    )(activations, output_grads, error_in.reshape(ys, depth, width), start_basis)
    return pl.pallas_call(
        write_kernel,
        out_shape=[
            jax.ShapeDtypeStruct((1, features, width), BF16),
            jax.ShapeDtypeStruct((features, width), BF16),
        ],
        in_specs=[in_vmem] * 3,
        out_specs=[in_hbm] * 2,
        scratch_shapes=[
            pltpu.VMEM((ys, depth, width), BF16),
            pltpu.SemaphoreType.DMA((2 * ys,)),
        ],
        compiler_params=pltpu.CompilerParams(vmem_limit_bytes=16 * 2**20),
        name="write",
    )(new_error, whole, clip)


def solution(mesh):
    in_specs = (P("dp", None, None), P("dp", None, "mp"), P("dp", None, "mp"), P(None, "mp"))
    out_specs = (P("dp", None, "mp"), P(None, "mp"))
    return jax.shard_map(
        per_device, mesh=mesh, in_specs=in_specs, out_specs=out_specs, check_vma=False
    )
```

time: 800 us -> 64.2 us (0.08)
  waiting for transfers between devices: 742 us -> 0 us
  Pallas kernels: 0 us -> 63.5 us
  matrix products: 22 us -> 0 us
  between operations: 14.8 us -> 0.64 us
  blocking collectives: 9.01 us -> 0 us
  other arithmetic: 8.15 us -> 0 us
    psum x2 -> x0, waiting for transfers between devices: 742 us -> none  [the longest x1 471 us: per_device(): left_factor = lax.psum(left_term, ('dp', 'mp'))]
    pallas_call x0 -> x2, Pallas kernels: none -> 63.5 us  [the longest x1 61.3 us: per_device(): pl.pallas_call(functools.partial(reduce_kernel, xs, ys, zs, cs, limit), o...]
    dot_general x5 -> x0, matrix products: 20.6 us -> none  [the longest x1 6.91 us: per_device(): lax.dot_general(ortho_basis, right_factor, (((0,), (0,)), ((), ())), prec...]
    psum x1 -> x0, blocking collectives: 9.01 us -> none  [per_device(): squares = lax.psum(jnp.sum(right_factor * right_factor), 'mp')]
  transfers between devices with their start and end apart: 2 -> 0, of which waited for: 2 -> 0; matrix products, arithmetic and copies ran while one was open for 0% -> 0% of each run, Pallas kernels for 0% -> 0%
where the time goes in v2:
time: 64.2 us; the launch traced here: 64.1 us
  Pallas kernels  63.5 us (99%)
    pallas_call x1, Pallas kernels, per_device(): pl.pallas_call(functools.partial(reduce_kernel, xs, ys, zs, cs, limit), o...  61.3 us
    pallas_call x1, Pallas kernels, per_device(): pl.pallas_call(write_kernel, out_shape=[jax.ShapeDtypeStruct((1, features...  2.14 us

profile of v2, /device:TPU:1, one launch (start us, length us, event | category | flops | bytes accessed | tf_op | source)
XLA Modules:
  0.0 64.1 jit_solution(7621985384373729956)
XLA Ops:
  0.6 61.3 %reduce.1 = (bf16[8,256,512]{2,1,0:T(8,128)(2,1)S(1)}, f32[8,256,512]{2,1,0:T(8,128)S(1)}, f32[8,128]{1,0:T(8,128)S(1)}) custom-call(bf16[1,256,2048]{2,1,0:T(8,128)(2,1)} %act_hbm.1, bf16[1,256,512]{2,1,0:T(8,128)(2,1)} %grad_hbm.1, bf16[8,256,512]{2,1,0:T(8,128)(2,1)} %bitcast.1, f32[32,512]{1,0:T(8,128)} %basis_hbm.1), custom_call_target="tpu_custom_call" | custom-call | tf_op jit(solution)/shard_map/reduce/pallas_call | solution.py:300
  62.0 2.1 %write.1 = (bf16[1,2048,512]{2,1,0:T(8,128)(2,1)}, bf16[2048,512]{1,0:T(8,128)(2,1)}) custom-call(bf16[8,256,512]{2,1,0:T(8,128)(2,1)S(1)} %get-tuple-element.5.err_in, f32[8,256,512]{2,1,0:T(8,128)S(1)} %get-tuple-element.6.whole, f32[8,128]{1,0:T(8,128)S(1)} %get-tuple-element.7.clip), custom_call_target="tpu_custom_call" | custom-call | tf_op jit(solution)/shard_map/write/pallas_call | solution.py:337

commit v3 on v2

--- a/solution.py
+++ b/solution.py
@@ -79,7 +79,8 @@
     in_sem, send_sem, recv_sem,
 ):
     replica, x = lax.axis_index("dp"), lax.axis_index("mp")
-    y, z, c = replica // (zs * cs), (replica // cs) % zs, replica % cs
+    y, rest = lax.div(replica, zs * cs), lax.rem(replica, zs * cs)
+    z, c = lax.div(rest, cs), lax.rem(rest, cs)
     ranks, width = basis.shape
     depth = act.shape[2]
     half = depth // cs
@@ -88,9 +89,12 @@
     def at(px, py, pz, pc):
         return ((py * zs + pz) * cs + pc, px)
 
-    plane = [((x + ox) % xs, (y + oy) % ys, ring(oy, ys)) for ox, oy in ring_offsets((xs, ys))]
-    column = [(y + oy) % ys for (oy,) in ring_offsets((ys,))]
-    line = [(z + oz) % zs for (oz,) in ring_offsets((zs,))]
+    along_x = [lax.rem(x + ox, xs) for ox in range(xs)]
+    along_y = [lax.rem(y + oy, ys) for oy in range(ys)]
+    along_z = [lax.rem(z + oz, zs) for oz in range(zs)]
+    plane = [(along_x[ox], along_y[oy], ring(oy, ys)) for ox, oy in ring_offsets((xs, ys))]
+    column = [along_y[oy] for (oy,) in ring_offsets((ys,))]
+    line = [along_z[oz] for (oz,) in ring_offsets((zs,))]
     twin = at(x, y, z, 1 - c)
     partners = [at(x, y, pz, c) for pz in line[:3]] + [at(px, py, z, c) for px, py, _ in plane]
     partners += [at(x, y, pz, c) for pz in line[3:]] + [twin]
@@ -98,19 +102,17 @@
     for partner in partners:
         pl.semaphore_signal(barrier, inc=1, device_id=partner, device_id_type=MESH)
 
-    loads = []
-
-    def load(source, target):
-        copy = pltpu.make_async_copy(source, target, in_sem.at[len(loads)])
-        copy.start()
-        loads.append(copy)
-
-    load(basis_hbm, basis)
-    load(grad_hbm.at[0], grad)
-    for py in range(ys):
-        load(act_hbm.at[0, :, pl.ds(py * depth, depth)], act.at[py])
-    for py in range(ys):
-        load(err_hbm.at[py], err.at[py])
+    def load(source, target, k):
+        pltpu.make_async_copy(source, target, in_sem.at[k]).start()
+
+    def loaded(target, k):
+        pltpu.make_async_copy(target, target, in_sem.at[k]).wait()
+
+    load(basis_hbm, basis, 0)
+    load(grad_hbm.at[0], grad, 1)
+    for py in range(ys):
+        load(act_hbm.at[0, :, pl.ds(py * depth, depth)], act.at[py], 2)
+    load(err_hbm, err, 3)
 
     def send(source, target, phase, device, arrival=None):
         pltpu.make_async_remote_copy(
@@ -128,13 +130,13 @@
     def sent(phase, like):
         pltpu.make_async_copy(like, like, send_sem.at[phase]).wait()
 
-    loads[0].wait()
-    loads[1].wait()
+    loaded(basis, 0)
+    loaded(grad, 1)
     basis_parts = stack(basis[...])
     through = stack(unstack(dot(basis_parts, grad[...], NT)))
-    for py in range(ys):
-        loads[2 + py].wait()
-        loads[2 + ys + py].wait()
+    loaded(act, 2)
+    loaded(err, 3)
+    for py in range(ys):
         term = unstack(dot(through, act[py], NN) + dot(basis_parts, err[py], NT))
         for h in range(cs):
             a_term[h, py] = term[:, h * half : (h + 1) * half].reshape(a_term.shape[2:])
@@ -166,19 +168,19 @@
 
     through = jnp.zeros((3 * ranks, grad.shape[0]), F32)
     term = jnp.zeros((3 * ranks, width), F32)
-    for distance in range(far + 2):
+    for distance in range(far + 3):
         if distance <= far:
             rows = [oy for oy in range(ys) if ring(oy, ys) == distance]
             count = len(rows) * xs - (distance == 0)
             arrived(PHASES + distance, a_split.at[pl.ds(0, count)])
             for oy in rows:
-                mine = left.at[c, (y + oy) % ys]
+                mine = left.at[c, along_y[oy]]
                 send(mine, mine, A_TWIN, twin, PHASES + far + 1 + distance)
-        if distance > 0:
-            rows = [oy for oy in range(ys) if ring(oy, ys) == distance - 1]
-            arrived(PHASES + far + distance, a_split.at[pl.ds(0, len(rows) * xs)])
+        if distance > 1:
+            rows = [oy for oy in range(ys) if ring(oy, ys) == distance - 2]
+            arrived(PHASES + far + distance - 1, a_split.at[pl.ds(0, len(rows) * xs)])
             for oy in rows:
-                py = (y + oy) % ys
+                py = along_y[oy]
                 block = stack(left_block(py))
                 through += dot(block, act[py], NT)
                 term += dot(block, err[py], NN)
@@ -325,7 +327,7 @@
             pltpu.VMEM(b_piece, F32),
             pltpu.VMEM((ys,) + b_piece, F32),
             pltpu.VMEM((ys * xs, ROWS, LANES), F32),
-            pltpu.SemaphoreType.DMA((2 + 2 * ys,)),
+            pltpu.SemaphoreType.DMA((4,)),
             pltpu.SemaphoreType.DMA((PHASES,)),
             pltpu.SemaphoreType.DMA((PHASES + 2 * (ys // 2 + 1),)),
         ],

time: 64.2 us -> 63.7 us (level)
  no operation moved by 1% of the time
where the time goes in v3:
time: 63.7 us; the launch traced here: 63.5 us
  Pallas kernels  62.9 us (99%)
  between operations  0.64 us (1%)
    pallas_call x1, Pallas kernels, per_device(): pl.pallas_call(functools.partial(reduce_kernel, xs, ys, zs, cs, limit), o...  60.8 us
    pallas_call x1, Pallas kernels, per_device(): pl.pallas_call(write_kernel, out_shape=[jax.ShapeDtypeStruct((1, features...  2.14 us

profile of v3, /device:TPU:1, one launch (start us, length us, event | category | flops | bytes accessed | tf_op | source)
XLA Modules:
  0.0 63.5 jit_solution(15787988768635697540)
XLA Ops:
  0.6 60.8 %reduce.1 = (bf16[8,256,512]{2,1,0:T(8,128)(2,1)S(1)}, f32[8,256,512]{2,1,0:T(8,128)S(1)}, f32[8,128]{1,0:T(8,128)S(1)}) custom-call(bf16[1,256,2048]{2,1,0:T(8,128)(2,1)} %act_hbm.1, bf16[1,256,512]{2,1,0:T(8,128)(2,1)} %grad_hbm.1, bf16[8,256,512]{2,1,0:T(8,128)(2,1)} %bitcast.1, f32[32,512]{1,0:T(8,128)} %basis_hbm.1), custom_call_target="tpu_custom_call" | custom-call | tf_op jit(solution)/shard_map/reduce/pallas_call | solution.py:302
  61.4 2.1 %write.1 = (bf16[1,2048,512]{2,1,0:T(8,128)(2,1)}, bf16[2048,512]{1,0:T(8,128)(2,1)}) custom-call(bf16[8,256,512]{2,1,0:T(8,128)(2,1)S(1)} %get-tuple-element.5.err_in, f32[8,256,512]{2,1,0:T(8,128)S(1)} %get-tuple-element.6.whole, f32[8,128]{1,0:T(8,128)S(1)} %get-tuple-element.7.clip), custom_call_target="tpu_custom_call" | custom-call | tf_op jit(solution)/shard_map/write/pallas_call | solution.py:339

commit v4 on v3

--- a/solution.py
+++ b/solution.py
@@ -70,9 +70,9 @@
 
 
 def reduce_kernel(
-    xs, ys, zs, cs, limit,
+    xs, ys, zs, cs,
     act_hbm, grad_hbm, err_hbm, basis_hbm,
-    err_out, whole_out, clip_out,
+    err_out, whole_out, total_out,
     act, grad, err, basis, acc,
     a_term, a_core, a_split, a_line, left, left_t,
     b_term, b_split, b_line, b_mine, b_core, right, norm,
@@ -230,9 +230,9 @@
         send(right.at[y], right.at[y], B_JOIN, at(x, py, z, c))
 
     factor = exact_dot(inverse, unpack(right[y], columns), NN)
-    squares = jnp.sum((factor * factor).reshape(ranks // ROWS, ROWS, columns), axis=0)
+    squares = jnp.sum(factor * factor, axis=0, keepdims=True)
     if columns < LANES:
-        squares = jnp.concatenate([squares, jnp.zeros((ROWS, LANES - columns), F32)], axis=1)
+        squares = jnp.concatenate([squares, jnp.zeros((1, LANES - columns), F32)], axis=1)
     else:
         squares = sum(squares[:, j : j + LANES] for j in range(0, columns, LANES))
     norm[me] = squares
@@ -250,12 +250,6 @@
         whole = dot(left_t[py], weights, NN)
         err_out[py] = (acc[py] - whole / replicas).astype(BF16)
         whole_out[py] = whole
-
-    arrived(NORM, norm.at[pl.ds(0, others)])
-    total = jnp.sum(norm[...], axis=0)
-    total = jnp.sum(jnp.sum(total, axis=0, keepdims=True), axis=1, keepdims=True)
-    ratio = jnp.sqrt(total) / limit
-    clip_out[...] = jnp.broadcast_to(1.0 / jnp.sqrt(1.0 + ratio * ratio), clip_out.shape)
 
     sent(A_CORE, a_core)
     sent(A_SPLIT, a_split.at[pl.ds(0, others)])
@@ -267,9 +261,11 @@
     sent(B_CORE, b_core)
     sent(B_JOIN, right.at[pl.ds(0, ys - 1)])
     sent(NORM, norm.at[pl.ds(0, others)])
-
-
-def write_kernel(err_in, whole, clip, err_hbm, upd_hbm, upd, sem):
+    arrived(NORM, norm.at[pl.ds(0, others)])
+    total_out[...] = jnp.sum(norm[...], axis=0)
+
+
+def write_kernel(limit, err_in, whole, total, err_hbm, upd_hbm, upd, sem):
     blocks, depth, width = whole.shape
     copies = []
 
@@ -279,9 +275,10 @@
 
     for k in range(blocks):
         store(err_in.at[k], err_hbm.at[0, pl.ds(k * depth, depth)])
-    scale = clip[:1, :1]
+    ratio = jnp.sqrt(jnp.sum(total[...], axis=1, keepdims=True)) / limit
+    clip = 1.0 / jnp.sqrt(1.0 + ratio * ratio)
     for k in range(blocks):
-        upd[k] = (scale * whole[k]).astype(BF16)
+        upd[k] = (clip * whole[k]).astype(BF16)
         store(upd.at[k], upd_hbm.at[pl.ds(k * depth, depth)])
     for copy in copies:
         copy.wait()
@@ -299,12 +296,12 @@
     b_piece = (ROWS, ranks // ROWS * (width // ys))
     in_vmem = pl.BlockSpec(memory_space=pltpu.VMEM)
     in_hbm = pl.BlockSpec(memory_space=pl.ANY)
-    new_error, whole, clip = pl.pallas_call(
-        functools.partial(reduce_kernel, xs, ys, zs, cs, limit),
+    new_error, whole, total = pl.pallas_call(
+        functools.partial(reduce_kernel, xs, ys, zs, cs),
         out_shape=[
             pltpu.VMEM((ys, depth, width), BF16),
             pltpu.VMEM((ys, depth, width), F32),
-            pltpu.VMEM((ROWS, LANES), F32),
+            pltpu.VMEM((1, LANES), F32),
         ],
         in_specs=[in_hbm] * 4,
         out_specs=[in_vmem] * 3,
@@ -326,7 +323,7 @@
             pltpu.VMEM(b_piece, F32),
             pltpu.VMEM(b_piece, F32),
             pltpu.VMEM((ys,) + b_piece, F32),
-            pltpu.VMEM((ys * xs, ROWS, LANES), F32),
+            pltpu.VMEM((ys * xs, 1, LANES), F32),
             pltpu.SemaphoreType.DMA((4,)),
             pltpu.SemaphoreType.DMA((PHASES,)),
             pltpu.SemaphoreType.DMA((PHASES + 2 * (ys // 2 + 1),)),
@@ -337,7 +334,7 @@
         name="reduce",
     )(activations, output_grads, error_in.reshape(ys, depth, width), start_basis)
     return pl.pallas_call(
-        write_kernel,
+        functools.partial(write_kernel, limit),
         out_shape=[
             jax.ShapeDtypeStruct((1, features, width), BF16),
             jax.ShapeDtypeStruct((features, width), BF16),
@@ -350,7 +347,7 @@
         ],
         compiler_params=pltpu.CompilerParams(vmem_limit_bytes=16 * 2**20),
         name="write",
-    )(new_error, whole, clip)
+    )(new_error, whole, total)
 
 
 def solution(mesh):

time: 63.7 us -> 62.3 us (0.978)
  Pallas kernels: 62.9 us -> 61.6 us
    pallas_call x2, Pallas kernels: 62.9 us -> 61.6 us  [the longest x1 59.4 us: per_device(): pl.pallas_call(functools.partial(reduce_kernel, xs, ys, zs, cs), out_shap...]
where the time goes in v4:
time: 62.3 us; the launch traced here: 62.2 us
  Pallas kernels  61.6 us (99%)
  between operations  0.64 us (1%)
    pallas_call x1, Pallas kernels, per_device(): pl.pallas_call(functools.partial(reduce_kernel, xs, ys, zs, cs), out_shap...  59.4 us
    pallas_call x1, Pallas kernels, per_device(): pl.pallas_call(functools.partial(write_kernel, limit), out_shape=[jax.Sha...  2.14 us

profile of v4, /device:TPU:1, one launch (start us, length us, event | category | flops | bytes accessed | tf_op | source)
XLA Modules:
  0.0 62.2 jit_solution(503463000799548075)
XLA Ops:
  0.6 59.4 %reduce.1 = (bf16[8,256,512]{2,1,0:T(8,128)(2,1)S(1)}, f32[8,256,512]{2,1,0:T(8,128)S(1)}, f32[1,128]{1,0:T(1,128)S(1)}) custom-call(bf16[1,256,2048]{2,1,0:T(8,128)(2,1)} %act_hbm.1, bf16[1,256,512]{2,1,0:T(8,128)(2,1)} %grad_hbm.1, bf16[8,256,512]{2,1,0:T(8,128)(2,1)} %bitcast.1, f32[32,512]{1,0:T(8,128)} %basis_hbm.1), custom_call_target="tpu_custom_call" | custom-call | tf_op jit(solution)/shard_map/reduce/pallas_call | solution.py:299
  60.1 2.1 %write.1 = (bf16[1,2048,512]{2,1,0:T(8,128)(2,1)}, bf16[2048,512]{1,0:T(8,128)(2,1)}) custom-call(bf16[8,256,512]{2,1,0:T(8,128)(2,1)S(1)} %get-tuple-element.5.err_in, f32[8,256,512]{2,1,0:T(8,128)S(1)} %get-tuple-element.6.whole, f32[1,128]{1,0:T(1,128)S(1)} %get-tuple-element.7.total), custom_call_target="tpu_custom_call" | custom-call | tf_op jit(solution)/shard_map/write/pallas_call | solution.py:336

commit v5 on v4

--- a/solution.py
+++ b/solution.py
@@ -267,21 +267,19 @@
 
 def write_kernel(limit, err_in, whole, total, err_hbm, upd_hbm, upd, sem):
     blocks, depth, width = whole.shape
-    copies = []
-
-    def store(source, target):
-        copies.append(pltpu.make_async_copy(source, target, sem.at[len(copies)]))
-        copies[-1].start()
+
+    def rows(k):
+        return pl.ds(k * depth, depth)
 
     for k in range(blocks):
-        store(err_in.at[k], err_hbm.at[0, pl.ds(k * depth, depth)])
+        pltpu.make_async_copy(err_in.at[k], err_hbm.at[0, rows(k)], sem.at[0]).start()
     ratio = jnp.sqrt(jnp.sum(total[...], axis=1, keepdims=True)) / limit
     clip = 1.0 / jnp.sqrt(1.0 + ratio * ratio)
     for k in range(blocks):
         upd[k] = (clip * whole[k]).astype(BF16)
-        store(upd.at[k], upd_hbm.at[pl.ds(k * depth, depth)])
-    for copy in copies:
-        copy.wait()
+        pltpu.make_async_copy(upd.at[k], upd_hbm.at[rows(k)], sem.at[1]).start()
+    pltpu.make_async_copy(err_in, err_in, sem.at[0]).wait()
+    pltpu.make_async_copy(upd, upd, sem.at[1]).wait()
 
 
 def per_device(activations, output_grads, error_in, start_basis):
@@ -343,7 +341,7 @@
         out_specs=[in_hbm] * 2,
         scratch_shapes=[
             pltpu.VMEM((ys, depth, width), BF16),
-            pltpu.SemaphoreType.DMA((2 * ys,)),
+            pltpu.SemaphoreType.DMA((2,)),
         ],
         compiler_params=pltpu.CompilerParams(vmem_limit_bytes=16 * 2**20),
         name="write",

time: 62.3 us -> 62.2 us (level)
  no operation moved by 1% of the time
where the time goes in v5:
time: 62.2 us; the launch traced here: 62.1 us
  Pallas kernels  61.4 us (99%)
  between operations  0.64 us (1%)
    pallas_call x1, Pallas kernels, per_device(): pl.pallas_call(functools.partial(reduce_kernel, xs, ys, zs, cs), out_shap...  59.4 us
    pallas_call x1, Pallas kernels, per_device(): pl.pallas_call(functools.partial(write_kernel, limit), out_shape=[jax.Sha...  2.01 us

profile of v5, /device:TPU:1, one launch (start us, length us, event | category | flops | bytes accessed | tf_op | source)
XLA Modules:
  0.0 62.1 jit_solution(16940335293755608163)
XLA Ops:
  0.6 59.4 %reduce.1 = (bf16[8,256,512]{2,1,0:T(8,128)(2,1)S(1)}, f32[8,256,512]{2,1,0:T(8,128)S(1)}, f32[1,128]{1,0:T(1,128)S(1)}) custom-call(bf16[1,256,2048]{2,1,0:T(8,128)(2,1)} %act_hbm.1, bf16[1,256,512]{2,1,0:T(8,128)(2,1)} %grad_hbm.1, bf16[8,256,512]{2,1,0:T(8,128)(2,1)} %bitcast.1, f32[32,512]{1,0:T(8,128)} %basis_hbm.1), custom_call_target="tpu_custom_call" | custom-call | tf_op jit(solution)/shard_map/reduce/pallas_call | solution.py:297
  60.1 2.0 %write.1 = (bf16[1,2048,512]{2,1,0:T(8,128)(2,1)}, bf16[2048,512]{1,0:T(8,128)(2,1)}) custom-call(bf16[8,256,512]{2,1,0:T(8,128)(2,1)S(1)} %get-tuple-element.5.err_in, f32[8,256,512]{2,1,0:T(8,128)S(1)} %get-tuple-element.6.whole, f32[1,128]{1,0:T(1,128)S(1)} %get-tuple-element.7.total), custom_call_target="tpu_custom_call" | custom-call | tf_op jit(solution)/shard_map/write/pallas_call | solution.py:334
